TPU v7x, 256 devices: a whole 4x4x8 slice. The times are simulated.
256 devices in a mesh: dp: 128 (over x, y, z), group: 2 (over core).
Axes of the slice: x: 4, y: 4, z: 8, core: 2. Of those that a mesh axis runs over, the one named last changes fastest.
Arguments:
- tokens_in: bfloat16 [128, 256, 1536], P('dp', None, 'group'), may hold values from -24 to 24
- dw_kernel: float32 [7, 1536], P(None, 'group'), may hold values from -2 to 2
- point_weight: bfloat16 [1536, 1536], P(None, 'group'), may hold values from -0.15625 to 0.15625
- positive_emb: bfloat16 [128, 1536], P('dp', 'group'), may hold values from -0.15625 to 0.15625
- bank: bfloat16 [16384, 1536], P('dp', 'group'), may hold values from -0.15625 to 0.15625
- neg_owner: int32 [16384, 1], P('dp'), may hold values from 0 to 127; in each aligned block of 128 rows (0 to 127, 128 to 255, ...) at most 2 rows name the same one
- neg_block: int32 [16384], P('dp'), may hold values from 0 to 15
Outputs:
- grad_bank: float32 [16384, 1536], P('dp', 'group')
- grad_kernel: float32 [7, 1536], P(None, 'group')
- grad_weight: float32 [1536, 1536], P('dp', 'group')
Inputs may be any that keep to these rules, and one draw needn't show every extreme that they name: `neg_owner`: among the 128 requests of one batch shard (aligned blocks of 128 rows), no owner is named more than 2 times.
All inputs are finite; a program needn't handle non-finite values.
Results may differ from a plain program's by a relative error of at most 0.0036.
Values may be sent and summed in bfloat16 or wider, within the bound.
No kernel may reach another device: no remote copies, remote signals or barrier semaphores. Data moves between devices by JAX's collectives and lax.ppermute only.
A program may use at most 128 MiB of HBM per device.

v0:
```python
import jax
import jax.numpy as jnp
from jax import lax
from jax.sharding import PartitionSpec as P

ROWS = 8
CAP = 2
SOFTMAX_TEMPER = 0.07
LOSS_SCALE = 256.0
EPSILON = 1e-06
PRECISE = lax.Precision.HIGHEST


def depthwise(tokens, kernel):
    margin = kernel.shape[0] // 2
    seq_length = tokens.shape[1]
    padded = jnp.pad(tokens.astype(jnp.float32), ((0, 0), (margin, margin), (0, 0)))
    running_sum = jnp.zeros(tokens.shape, jnp.float32)
    for tap_index in range(kernel.shape[0]):
        running_sum = (
            running_sum + kernel[tap_index] * padded[:, tap_index : tap_index + seq_length, :]
        )
    return (running_sum, padded)


def kernel_term(grad_hidden, padded, tap_count):
    seq_length = grad_hidden.shape[1]
    return jnp.stack(
        [
            jnp.sum(grad_hidden * padded[:, tap_index : tap_index + seq_length, :], axis=(0, 1))
            for tap_index in range(tap_count)
        ]
    )


def gelu_back(mixed_out, cotangent):
    return jax.vjp(lambda entry_value: jax.nn.gelu(entry_value, approximate=True), mixed_out)[1](
        cotangent
    )[0]


def per_device(tokens_in, dw_kernel, point_weight, positive_emb, bank, neg_owner, neg_block):
    seq_count, seq_length, half_width = tokens_in.shape
    token_count = seq_count * seq_length
    device_count = lax.axis_size("dp")
    slot_count = device_count * CAP
    block_count = bank.shape[0] // ROWS
    request_count = neg_owner.shape[0]
    local_rows = bank.shape[0]
    local_end = seq_count + local_rows
    hidden_f, padded = depthwise(tokens_in, dw_kernel)
    hidden = hidden_f.astype(jnp.bfloat16).reshape(token_count, half_width)
    mixed_part = lax.dot_general(
        hidden, point_weight, (((1,), (1,)), ((), ())), preferred_element_type=jnp.float32
    )
    mixed_out = lax.psum_scatter(mixed_part, "group", scatter_dimension=1, tiled=True)
    activated = jax.nn.gelu(mixed_out, approximate=True)
    embedding = jnp.mean(
        tokens_in.astype(jnp.float32) + activated.reshape(seq_count, seq_length, half_width), axis=1
    )
    owners = neg_owner[:, 0]
    owner_hits = (owners[:, None] == jnp.arange(device_count, dtype=jnp.int32)[None, :]).astype(
        jnp.int32
    )
    earlier = jnp.cumsum(owner_hits, axis=0) - owner_hits
    rank_in_owner = jnp.sum(earlier * owner_hits, axis=1)
    slot_index = owners * CAP + rank_in_owner
    slot_hits = (slot_index[:, None] == jnp.arange(slot_count, dtype=jnp.int32)[None, :]).astype(
        jnp.int32
    )
    wanted = jnp.sum(slot_hits * (neg_block[:, None] + 1), axis=0) - 1
    asked_blocks = lax.all_to_all(
        wanted.reshape(device_count, CAP), "dp", split_axis=0, concat_axis=0, tiled=True
    )
    asked_flat = asked_blocks.reshape(slot_count)
    blocks_local = bank.reshape(block_count, ROWS, half_width)
    served = jnp.take(blocks_local, jnp.maximum(asked_flat, 0), axis=0)
    served = jnp.where((asked_flat >= 0)[:, None, None], served, jnp.zeros((), jnp.bfloat16))
    fetched = lax.all_to_all(
        served.reshape(device_count, CAP, ROWS, half_width),
        "dp",
        split_axis=0,
        concat_axis=0,
        tiled=True,
    )
    negatives = jnp.take(fetched.reshape(slot_count, ROWS, half_width), slot_index, axis=0).reshape(
        request_count * ROWS, half_width
    )
    key_rows = jnp.concatenate([positive_emb, bank, negatives], axis=0)
    column_count = key_rows.shape[0]
    key_float = key_rows.astype(jnp.float32)
    dots_part = lax.dot_general(embedding, key_float, (((1,), (1,)), ((), ())), precision=PRECISE)
    inner_products, embed_sq, key_sq = lax.psum(
        (dots_part, jnp.sum(embedding * embedding, axis=1), jnp.sum(key_float * key_float, axis=1)),
        "group",
    )
    embedding_norm = jnp.sqrt(embed_sq + EPSILON)
    key_length_norm = jnp.sqrt(key_sq + EPSILON)
    score_matrix = inner_products / (
        SOFTMAX_TEMPER * embedding_norm[:, None] * key_length_norm[None, :]
    )
    exponent = jnp.exp(score_matrix)
    weights = exponent / jnp.sum(exponent, axis=1, keepdims=True)
    score_gradient = LOSS_SCALE * (weights - jnp.eye(seq_count, column_count, dtype=jnp.float32))
    blend_factor = score_gradient / (SOFTMAX_TEMPER * key_length_norm[None, :])
    unit_query = embedding / embedding_norm[:, None]
    row_weight = jnp.sum(score_gradient * score_matrix, axis=1)
    column_weight = jnp.sum(score_gradient * score_matrix, axis=0)
    key_scale = column_weight / (key_length_norm * key_length_norm)
    query_dir = jnp.dot(blend_factor, key_float, precision=PRECISE)
    embed_grad = (query_dir - row_weight[:, None] * unit_query) / embedding_norm[:, None]
    key_grad = (
        lax.dot_general(blend_factor, unit_query, (((0,), (0,)), ((), ())), precision=PRECISE)
        - key_scale[:, None] * key_float
    )
    local_grad = key_grad[seq_count:local_end]
    neg_grad = key_grad[local_end:].reshape(request_count, ROWS, half_width)
    outgoing = jnp.zeros((slot_count, ROWS, half_width), jnp.float32).at[slot_index].set(neg_grad)
    returned = lax.all_to_all(
        outgoing.reshape(device_count, CAP, ROWS, half_width),
        "dp",
        split_axis=0,
        concat_axis=0,
        tiled=True,
    )
    block_pick = (asked_flat[:, None] == jnp.arange(block_count, dtype=jnp.int32)[None, :]).astype(
        jnp.float32
    )
    remote = lax.dot_general(
        block_pick,
        returned.reshape(slot_count, ROWS * half_width),
        (((0,), (0,)), ((), ())),
        precision=PRECISE,
    )
    bank_grad = local_grad + remote.reshape(local_rows, half_width)
    act_grad = jnp.broadcast_to(
        (embed_grad / seq_length)[:, None, :], (seq_count, seq_length, half_width)
    ).reshape(token_count, half_width)
    mixed_grad = gelu_back(mixed_out, act_grad).astype(jnp.bfloat16)
    mixed_all = lax.all_gather(mixed_grad, "group", axis=1, tiled=True)
    hidden_grad = jnp.dot(mixed_all, point_weight, preferred_element_type=jnp.float32)
    kernel_part = kernel_term(
        hidden_grad.reshape(seq_count, seq_length, half_width), padded, dw_kernel.shape[0]
    )
    kernel_grad = lax.psum(kernel_part, "dp") / device_count
    weight_grad = (
        lax.psum_scatter(
            lax.dot_general(
                mixed_all, hidden, (((0,), (0,)), ((), ())), preferred_element_type=jnp.float32
            ),
            "dp",
            scatter_dimension=0,
            tiled=True,
        )
        / device_count
    )
    return (bank_grad, kernel_grad, weight_grad)


def solution(mesh):
    in_specs = (
        P("dp", None, "group"),
        P(None, "group"),
        P(None, "group"),
        P("dp", "group"),
        P("dp", "group"),
        P("dp", None),
        P("dp"),
    )
    out_specs = (P("dp", "group"), P(None, "group"), P("dp", "group"))
    return jax.shard_map(
        per_device, mesh=mesh, in_specs=in_specs, out_specs=out_specs, check_vma=False
    )
```

profile of v0, /device:TPU:54, one launch (start us, length us, event | category | flops | bytes accessed | tf_op | source)
XLA Modules:
  0.0 1563.4 jit_solution(61074231811996590)
XLA Ops:
  10.7 22.3 %all_to_all.16 = s32[128,1,2]{2,1,0:T(1,128)S(1)} all-to-all(s32[128,1,2]{2,1,0:T(1,128)S(1)} %bitcast.66), channel_id=1, replica_groups=mesh['dp'=128,'group'=2] {'dp'}, dimensions={0} | all-to-all | bytes 2048 | tf_op jit(solution)/shard_map/all_to_all | solution.py:72
  33.6 3.4 gather_fusion
  37.0 3.5 select_select_fusion
  40.5 11.9 all-to-all-start.1
  54.1 2.0 fusion.14
  56.3 15.2 reduce-scatter.4.cloned.1.call-done
  71.4 1.5 fusion.10
  73.5 48.7 %all-to-all-done.1 = bf16[128,2,8,768]{3,2,1,0:T(8,128)(2,1)} async-done(((bf16[128,2,8,768]{3,2,1,0:T(8,128)(2,1)}), bf16[128,2,8,768]{3,2,1,0:T(8,128)(2,1)}, u32[]{:S(2)}, u32[]{:S(2)}) %all-to-all-start.1) | async-done | bytes 3145760 | tf_op jit(solution)/shard_map/all_to_all | solution.py:79
  122.2 3.7 gather_fusion.1
  126.0 2.8 bitcast_select_fusion
  128.8 10.8 concatenate.3
  139.6 1.9 fusion.1
  141.5 3.0 fusion.27
  144.5 4.5 all-reduce.3
  151.7 2.3 convolution_reduce_fusion
  155.3 1.7 copy-done.3
  157.0 1.9 slice_bitcast_fusion
  158.9 3.1 broadcast_in_dim.66
  161.9 18.4 %scatter_fusion = f32[256,8,768]{2,1,0:T(8,128)} fusion(f32[256,8,768]{2,1,0:T(8,128)} %broadcast_in_dim.66, s32[128]{0:T(128)S(1)} %get-tuple-element.37, f32[128,8,768]{2,1,0:T(8,128)} %slice_bitcast_fusion), kind=kCustom, calls=%fused_computation.2 | custom fusion | bytes 9437696 | tf_op jit(solution)/shard_map/scatter | solution.py:118
  180.3 13.1 all-to-all-start.2
  194.0 2.4 all_gather.3
  196.4 2.9 fusion.12
  199.3 462.3 %fusion = f32[16,768]{1,0:T(8,128)} fusion(f32[1536,768]{1,0:T(8,128)} %fusion.12), kind=kCustom, calls=%all-reduce-scatter | all-reduce-scatter fusion | flops 1572865 | bytes 4768768
  665.0 1.3 collective-permute-start.29
  666.3 1.3 collective-permute-start.28
  667.6 1.3 collective-permute-start.27
  671.6 1.3 collective-permute-start.25
  672.9 5.3 collective-permute-done.29
  678.2 1.3 collective-permute-start.24
  679.5 5.8 collective-permute-done.28
  685.3 1.3 collective-permute-start.23
  686.6 2.1 collective-permute-done.27
  690.0 4.7 collective-permute-done.26
  695.9 1.6 collective-permute-done.25
  698.8 3.3 collective-permute-done.24
  702.0 1.3 collective-permute-start.19
  703.3 7.4 collective-permute-done.23
  712.0 5.6 collective-permute-done.22
  718.8 8.3 collective-permute-done.21
  728.5 2.2 collective-permute-done.20
  731.9 2.5 collective-permute-done.19
  736.6 2.2 collective-permute-start.13
  738.8 2.6 collective-permute-start.12
  741.4 2.7 collective-permute-start.11
  744.1 1.9 collective-permute-start.10
  747.8 2.3 reduce.27
  751.0 1.9 collective-permute-start.9
  753.0 1.9 collective-permute-start.8
  754.9 1.9 collective-permute-start.7
  756.9 1.9 collective-permute-start.6
  758.8 1.9 collective-permute-start.5
  760.8 4.3 multiply_reduce_fusion
  765.2 672.5 %psum.31 = f32[7,768]{1,0:T(8,128)S(1)} all-reduce(f32[7,768]{1,0:T(8,128)S(1)} %stack.31), channel_id=1, replica_groups=mesh['dp'=128,'group'=2] {'dp'}, use_global_device_ids=true, to_apply=%region_20.21 | all-reduce | flops 5376 | bytes 43008 | tf_op jit(solution)/shard_map/psum | solution.py:145
  1437.7 15.9 %collective-permute-start.4 = (f32[16,768]{1,0:T(8,128)}, f32[16,768]{1,0:T(8,128)S(1)}, u32[]{:S(2)}, u32[]{:S(2)}) collective-permute-start(f32[16,768]{1,0:T(8,128)} %fusion), channel_id=1, source_target_pairs={{0,10},{2,12},{4,14},{6,16},{8,18},{10,20},{12,22},{14,24},{16,26}... | collective-permute-start | bytes 147464
  1453.6 15.1 collective-permute-start.3
  1468.8 13.4 collective-permute-start.2
  1482.2 8.8 collective-permute-start.1
  1491.0 2.1 collective-permute-start
  1493.8 3.4 collective-permute-done
  1497.2 48.4 %concatenate.4 = f32[524,768]{1,0:T(8,128)} concatenate(f32[12,768]{1,0:T(8,128)} %copy-done.9, f32[16,768]{1,0:T(8,128)} %collective-permute-done.30, f32[16,768]{1,0:T(8,128)} %collective-permute-done.29, f32[16,768]{1,0:T(8,128)} %collective-permute-done.28, f32[16,768]{1,0:T(8,128)} %collective-permute-done.27, f32[16,768]{1,0:T(8,128)} %collective-permute-done.26, ...), dimensions={0} | concatenate | bytes 3219456
  1545.7 1.5 dynamic-slice_multiply_fusion
  1547.2 5.4 copy.27
  1552.6 2.2 fusion.16
  1554.8 1.8 slice_add_fusion
  (108 shorter events, 30.2 us)
Async XLA Ops:
  7.2 46.9 %copy-start = (bf16[1536,768]{1,0:T(8,128)(2,1)S(1)}, bf16[1536,768]{1,0:T(8,128)(2,1)}, u32[]{:S(2)}) copy-start(bf16[1536,768]{1,0:T(8,128)(2,1)} %param.9) | copy-start | bytes 7077892
  33.0 4.0 copy-start.8
  40.5 11.9 copy-start.6
  40.5 12.0 copy-start.10
  40.5 81.8 %all-to-all-start.1 = ((bf16[128,2,8,768]{3,2,1,0:T(8,128)(2,1)}), bf16[128,2,8,768]{3,2,1,0:T(8,128)(2,1)}, u32[]{:S(2)}, u32[]{:S(2)}) async-start(bf16[128,2,8,768]{3,2,1,0:T(8,128)(2,1)} %select_select_fusion), calls=%async_computation.2 | async-start | bytes 6291456 | tf_op jit(solution)/shard_map/all_to_all | solution.py:79
  52.4 19.1 %reduce-scatter.4.cloned.1.call-start = ((), (), s32[]{:S(2)}) async-start(), calls=%async_computation.4 | async-start | bytes 2359296 | tf_op jit(solution)/shard_map/reduce_scatter | solution.py:56
  52.5 0.9 copy-start.4
  54.0 2.0 copy-start.11
  122.2 6.5 copy-start.1
  122.2 6.5 copy-start.12
  148.9 5.8 copy-start.2
  155.2 1.7 copy-start.3
  180.3 13.2 copy-start.5
  180.3 1366.9 %all-to-all-start.2 = ((f32[128,2,8,768]{3,2,1,0:T(8,128)}), f32[128,2,8,768]{3,2,1,0:T(8,128)}, u32[]{:S(2)}, u32[]{:S(2)}) async-start(f32[128,2,8,768]{3,2,1,0:T(8,128)} %bitcast.63), calls=%async_computation.3 | async-start | bytes 12582912 | tf_op jit(solution)/shard_map/all_to_all | solution.py:119
  199.3 546.7 %copy-start.13 = (u32[256]{0:T(256)S(1)}, u32[256]{0:T(256)}, u32[]{:S(2)}) copy-start(u32[256]{0:T(256)} %constant.94) | copy-start | bytes 3076
  199.3 561.4 %copy-start.7 = (bf16[1,256,768]{2,1,0:T(8,128)(2,1)S(1)}, bf16[1,256,768]{2,1,0:T(8,128)(2,1)}, u32[]{:S(2)}) copy-start(bf16[1,256,768]{2,1,0:T(8,128)(2,1)} %param.7) | copy-start | bytes 1179652
  661.6 10.0 collective-permute-start.30
  663.7 6.0 collective-permute-start.31
  665.0 13.2 collective-permute-start.29
  666.3 19.0 %collective-permute-start.28 = (f32[16,768]{1,0:T(8,128)}, f32[16,768]{1,0:T(8,128)}, u32[]{:S(2)}, u32[]{:S(2)}) collective-permute-start(f32[16,768]{1,0:T(8,128)} %fusion), channel_id=1, source_target_pairs={{0,58},{2,60},{4,62},{6,64},{8,66},{10,68},{12,70},{14,72},{16,74}... | collective-permute-start | bytes 147464
  667.6 21.1 %collective-permute-start.27 = (f32[16,768]{1,0:T(8,128)}, f32[16,768]{1,0:T(8,128)}, u32[]{:S(2)}, u32[]{:S(2)}) collective-permute-start(f32[16,768]{1,0:T(8,128)} %fusion), channel_id=1, source_target_pairs={{0,56},{2,58},{4,60},{6,62},{8,64},{10,66},{12,68},{14,70},{16,72}... | collective-permute-start | bytes 147464
  669.7 0.6 copy-start.9
  670.3 24.3 %collective-permute-start.26 = (f32[16,768]{1,0:T(8,128)}, f32[16,768]{1,0:T(8,128)}, u32[]{:S(2)}, u32[]{:S(2)}) collective-permute-start(f32[16,768]{1,0:T(8,128)} %fusion), channel_id=1, source_target_pairs={{0,54},{2,56},{4,58},{6,60},{8,62},{10,64},{12,66},{14,68},{16,70}... | collective-permute-start | bytes 147464
  671.6 25.9 %collective-permute-start.25 = (f32[16,768]{1,0:T(8,128)}, f32[16,768]{1,0:T(8,128)}, u32[]{:S(2)}, u32[]{:S(2)}) collective-permute-start(f32[16,768]{1,0:T(8,128)} %fusion), channel_id=1, source_target_pairs={{0,52},{2,54},{4,56},{6,58},{8,60},{10,62},{12,64},{14,66},{16,68}... | collective-permute-start | bytes 147464
  678.2 23.8 %collective-permute-start.24 = (f32[16,768]{1,0:T(8,128)}, f32[16,768]{1,0:T(8,128)}, u32[]{:S(2)}, u32[]{:S(2)}) collective-permute-start(f32[16,768]{1,0:T(8,128)} %fusion), channel_id=1, source_target_pairs={{0,50},{2,52},{4,54},{6,56},{8,58},{10,60},{12,62},{14,64},{16,66}... | collective-permute-start | bytes 147464
  685.3 25.4 %collective-permute-start.23 = (f32[16,768]{1,0:T(8,128)}, f32[16,768]{1,0:T(8,128)}, u32[]{:S(2)}, u32[]{:S(2)}) collective-permute-start(f32[16,768]{1,0:T(8,128)} %fusion), channel_id=1, source_target_pairs={{0,48},{2,50},{4,52},{6,54},{8,56},{10,58},{12,60},{14,62},{16,64}... | collective-permute-start | bytes 147464
  688.7 28.9 %collective-permute-start.22 = (f32[16,768]{1,0:T(8,128)}, f32[16,768]{1,0:T(8,128)}, u32[]{:S(2)}, u32[]{:S(2)}) collective-permute-start(f32[16,768]{1,0:T(8,128)} %fusion), channel_id=1, source_target_pairs={{0,46},{2,48},{4,50},{6,52},{8,54},{10,56},{12,58},{14,60},{16,62}... | collective-permute-start | bytes 147464
  694.6 32.6 %collective-permute-start.21 = (f32[16,768]{1,0:T(8,128)}, f32[16,768]{1,0:T(8,128)}, u32[]{:S(2)}, u32[]{:S(2)}) collective-permute-start(f32[16,768]{1,0:T(8,128)} %fusion), channel_id=1, source_target_pairs={{0,44},{2,46},{4,48},{6,50},{8,52},{10,54},{12,56},{14,58},{16,60}... | collective-permute-start | bytes 147464
  697.5 33.2 %collective-permute-start.20 = (f32[16,768]{1,0:T(8,128)}, f32[16,768]{1,0:T(8,128)}, u32[]{:S(2)}, u32[]{:S(2)}) collective-permute-start(f32[16,768]{1,0:T(8,128)} %fusion), channel_id=1, source_target_pairs={{0,42},{2,44},{4,46},{6,48},{8,50},{10,52},{12,54},{14,56},{16,58}... | collective-permute-start | bytes 147464
  702.0 32.4 %collective-permute-start.19 = (f32[16,768]{1,0:T(8,128)}, f32[16,768]{1,0:T(8,128)}, u32[]{:S(2)}, u32[]{:S(2)}) collective-permute-start(f32[16,768]{1,0:T(8,128)} %fusion), channel_id=1, source_target_pairs={{0,40},{2,42},{4,44},{6,46},{8,48},{10,50},{12,52},{14,54},{16,56}... | collective-permute-start | bytes 147464
  710.7 25.9 %collective-permute-start.18 = (f32[16,768]{1,0:T(8,128)}, f32[16,768]{1,0:T(8,128)}, u32[]{:S(2)}, u32[]{:S(2)}) collective-permute-start(f32[16,768]{1,0:T(8,128)} %fusion), channel_id=1, source_target_pairs={{0,38},{2,40},{4,42},{6,44},{8,46},{10,48},{12,50},{14,52},{16,54}... | collective-permute-start | bytes 147464
  717.6 21.2 %collective-permute-start.17 = (f32[16,768]{1,0:T(8,128)}, f32[16,768]{1,0:T(8,128)}, u32[]{:S(2)}, u32[]{:S(2)}) collective-permute-start(f32[16,768]{1,0:T(8,128)} %fusion), channel_id=1, source_target_pairs={{0,36},{2,38},{4,40},{6,42},{8,44},{10,46},{12,48},{14,50},{16,52}... | collective-permute-start | bytes 147464
  727.2 14.2 collective-permute-start.16
  730.7 13.4 collective-permute-start.15
  734.5 16.6 %collective-permute-start.14 = (f32[16,768]{1,0:T(8,128)}, f32[16,768]{1,0:T(8,128)}, u32[]{:S(2)}, u32[]{:S(2)}) collective-permute-start(f32[16,768]{1,0:T(8,128)} %fusion), channel_id=1, source_target_pairs={{0,30},{2,32},{4,34},{6,36},{8,38},{10,40},{12,42},{14,44},{16,46}... | collective-permute-start | bytes 147464
  736.6 16.4 %collective-permute-start.13 = (f32[16,768]{1,0:T(8,128)}, f32[16,768]{1,0:T(8,128)}, u32[]{:S(2)}, u32[]{:S(2)}) collective-permute-start(f32[16,768]{1,0:T(8,128)} %fusion), channel_id=1, source_target_pairs={{0,28},{2,30},{4,32},{6,34},{8,36},{10,38},{12,40},{14,42},{16,44}... | collective-permute-start | bytes 147464
  738.8 16.1 %collective-permute-start.12 = (f32[16,768]{1,0:T(8,128)}, f32[16,768]{1,0:T(8,128)}, u32[]{:S(2)}, u32[]{:S(2)}) collective-permute-start(f32[16,768]{1,0:T(8,128)} %fusion), channel_id=1, source_target_pairs={{0,26},{2,28},{4,30},{6,32},{8,34},{10,36},{12,38},{14,40},{16,42}... | collective-permute-start | bytes 147464
  741.4 15.4 collective-permute-start.11
  744.1 14.7 collective-permute-start.10
  751.0 686.6 %collective-permute-start.9 = (f32[16,768]{1,0:T(8,128)}, f32[16,768]{1,0:T(8,128)}, u32[]{:S(2)}, u32[]{:S(2)}) collective-permute-start(f32[16,768]{1,0:T(8,128)} %fusion), channel_id=1, source_target_pairs={{0,20},{2,22},{4,24},{6,26},{8,28},{10,30},{12,32},{14,34},{16,36}... | collective-permute-start | bytes 147464
  753.0 700.6 %collective-permute-start.8 = (f32[16,768]{1,0:T(8,128)}, f32[16,768]{1,0:T(8,128)}, u32[]{:S(2)}, u32[]{:S(2)}) collective-permute-start(f32[16,768]{1,0:T(8,128)} %fusion), channel_id=1, source_target_pairs={{0,18},{2,20},{4,22},{6,24},{8,26},{10,28},{12,30},{14,32},{16,34}... | collective-permute-start | bytes 147464
  754.9 713.8 %collective-permute-start.7 = (f32[16,768]{1,0:T(8,128)}, f32[16,768]{1,0:T(8,128)}, u32[]{:S(2)}, u32[]{:S(2)}) collective-permute-start(f32[16,768]{1,0:T(8,128)} %fusion), channel_id=1, source_target_pairs={{0,16},{2,18},{4,20},{6,22},{8,24},{10,26},{12,28},{14,30},{16,32}... | collective-permute-start | bytes 147464
  756.9 725.3 %collective-permute-start.6 = (f32[16,768]{1,0:T(8,128)}, f32[16,768]{1,0:T(8,128)}, u32[]{:S(2)}, u32[]{:S(2)}) collective-permute-start(f32[16,768]{1,0:T(8,128)} %fusion), channel_id=1, source_target_pairs={{0,14},{2,16},{4,18},{6,20},{8,22},{10,24},{12,26},{14,28},{16,30}... | collective-permute-start | bytes 147464
  758.8 732.2 %collective-permute-start.5 = (f32[16,768]{1,0:T(8,128)}, f32[16,768]{1,0:T(8,128)}, u32[]{:S(2)}, u32[]{:S(2)}) collective-permute-start(f32[16,768]{1,0:T(8,128)} %fusion), channel_id=1, source_target_pairs={{0,12},{2,14},{4,16},{6,18},{8,20},{10,22},{12,24},{14,26},{16,28}... | collective-permute-start | bytes 147464
  1437.7 56.1 %collective-permute-start.4 = (f32[16,768]{1,0:T(8,128)}, f32[16,768]{1,0:T(8,128)S(1)}, u32[]{:S(2)}, u32[]{:S(2)}) collective-permute-start(f32[16,768]{1,0:T(8,128)} %fusion), channel_id=1, source_target_pairs={{0,10},{2,12},{4,14},{6,16},{8,18},{10,20},{12,22},{14,24},{16,26}... | collective-permute-start | bytes 147464
  1453.6 40.2 %collective-permute-start.3 = (f32[16,768]{1,0:T(8,128)}, f32[16,768]{1,0:T(8,128)S(1)}, u32[]{:S(2)}, u32[]{:S(2)}) collective-permute-start(f32[16,768]{1,0:T(8,128)} %fusion), channel_id=1, source_target_pairs={{0,8},{2,10},{4,12},{6,14},{8,16},{10,18},{12,20},{14,22},{16,24},... | collective-permute-start | bytes 147464
  1468.8 25.0 %collective-permute-start.2 = (f32[16,768]{1,0:T(8,128)}, f32[16,768]{1,0:T(8,128)S(1)}, u32[]{:S(2)}, u32[]{:S(2)}) collective-permute-start(f32[16,768]{1,0:T(8,128)} %fusion), channel_id=1, source_target_pairs={{0,6},{2,8},{4,10},{6,12},{8,14},{10,16},{12,18},{14,20},{16,22},{... | collective-permute-start | bytes 147464
  1482.2 11.6 collective-permute-start.1
  1491.0 6.2 collective-permute-start
Sparse Core Ops, SparseCore 0:
  56.2 15.2 reduce-scatter.3
where the time goes:
time: 1570 us; the launch traced here: 1560 us
  blocking collectives  1160 us (74%)
  starting transfers between devices  123 us (8%)
  waiting for transfers between devices  118 us (8%)
  local copies, waits for them, and re-layouts  102 us (6%)
  other arithmetic  24.1 us (2%)
  matrix products  16.6 us (1%)
  between operations  16.2 us (1%)
    psum x1, blocking collectives, per_device(): kernel_grad = lax.psum(kernel_part, 'dp') / device_count  672 us
    unnamed x1, blocking collectives  462 us
    unnamed x32, starting transfers between devices  97.5 us
    unnamed x32, local copies, waits for them, and re-layouts  58.4 us
    unnamed x33, waiting for transfers between devices  53.8 us
    all_to_all x1, waiting for transfers between devices, per_device(): lax.all_to_all(served.reshape(device_count, CAP, ROWS, half_width), 'dp',...  48.7 us
  transfers between devices with their start and end apart: 35, of which 16 were waited for; matrix products, arithmetic and copies ran while one was open for 34% of the time, Pallas kernels for 0%

commit v1 on v0

--- a/solution.py
+++ b/solution.py
@@ -1,3 +1,4 @@
+import functools
 import jax
 import jax.numpy as jnp
 from jax import lax
@@ -9,6 +10,14 @@
 LOSS_SCALE = 256.0
 EPSILON = 1e-06
 PRECISE = lax.Precision.HIGHEST
+
+
+def _note_thing(local_values, mesh_ax):
+    k_now = jnp.sum(lax.all_gather(local_values, axis_name=mesh_ax), axis=0)
+    return k_now
+
+
+_recover_series_all = functools.partial(_note_thing, mesh_ax="dp")
 
 
 def depthwise(tokens, kernel):
@@ -142,7 +151,7 @@
     kernel_part = kernel_term(
         hidden_grad.reshape(seq_count, seq_length, half_width), padded, dw_kernel.shape[0]
     )
-    kernel_grad = lax.psum(kernel_part, "dp") / device_count
+    kernel_grad = _recover_series_all(kernel_part) / device_count
     weight_grad = (
         lax.psum_scatter(
             lax.dot_general(

time: 1570 us -> 895 us (0.57)
  the two profiles are of different devices: /device:TPU:54 before, /device:TPU:8 now
where the time goes in v1:
time: 895 us; the launch traced here: 891 us
  blocking collectives  523 us (58%)
  starting transfers between devices  137 us (15%)
  local copies, waits for them, and re-layouts  102 us (11%)
  waiting for transfers between devices  70.1 us (8%)
  other arithmetic  24.8 us (3%)
  matrix products  16.7 us (2%)
  between operations  16.4 us (2%)
    unnamed x1, blocking collectives  490 us
    unnamed x32, starting transfers between devices  119 us
    unnamed x44, local copies, waits for them, and re-layouts  55.8 us
    all_to_all x1, waiting for transfers between devices, per_device(): lax.all_to_all(served.reshape(device_count, CAP, ROWS, half_width), 'dp',...  51 us
    all_to_all x1, blocking collectives, per_device(): lax.all_to_all(wanted.reshape(device_count, CAP), 'dp', split_axis=0, con...  26.2 us
    scatter x1, local copies, waits for them, and re-layouts, per_device(): jnp.zeros((slot_count, ROWS, half_width), jnp.float32).at[slot_index]  18.4 us
  transfers between devices with their start and end apart: 36, of which 4 were waited for; matrix products, arithmetic and copies ran while one was open for 63% of the time, Pallas kernels for 0%

profile of v1, /device:TPU:8, one launch (start us, length us, event | category | flops | bytes accessed | tf_op | source)
XLA Modules:
  0.0 890.7 jit_solution(12890750195773616874)
XLA Ops:
  10.7 26.2 %all_to_all.16 = s32[128,1,2]{2,1,0:T(1,128)S(1)} all-to-all(s32[128,1,2]{2,1,0:T(1,128)S(1)} %bitcast.67), channel_id=1, replica_groups=mesh['dp'=128,'group'=2] {'dp'}, dimensions={0} | all-to-all | bytes 2048 | tf_op jit(solution)/shard_map/all_to_all | solution.py:81
  37.5 3.4 gather_fusion
  40.9 3.5 select_select_fusion
  44.4 7.9 all-to-all-start.1
  54.0 2.0 fusion.14
  56.2 15.8 %reduce-scatter.4.cloned.1.call-done = f32[256,768]{1,0:T(8,128)} async-done(((f32[256,1536]{1,0:T(8,128)}), f32[256,768]{1,0:T(8,128)}) %reduce-scatter.4.cloned.1.call-update) | async-done | bytes 786448 | tf_op jit(solution)/shard_map/reduce_scatter | solution.py:65
  72.0 1.5 fusion.10
  74.0 51.0 %all-to-all-done.1 = bf16[128,2,8,768]{3,2,1,0:T(8,128)(2,1)} async-done(((bf16[128,2,8,768]{3,2,1,0:T(8,128)(2,1)}), bf16[128,2,8,768]{3,2,1,0:T(8,128)(2,1)}, u32[]{:S(2)}, u32[]{:S(2)}) %all-to-all-start.1) | async-done | bytes 3145760 | tf_op jit(solution)/shard_map/all_to_all | solution.py:88
  125.0 3.7 gather_fusion.1
  128.7 2.8 bitcast_select_fusion
  131.5 10.8 %concatenate.3 = bf16[1153,768]{1,0:T(8,128)(2,1)} concatenate(bf16[1,768]{1,0:T(2,128)(2,1)S(1)} %copy-done.18, bf16[128,768]{1,0:T(8,128)(2,1)S(1)} %copy-done.1, bf16[1024,768]{1,0:T(8,128)(2,1)} %bitcast_select_fusion), dimensions={0} | concatenate | bytes 3542016 | tf_op jit(solution)/shard_map/concatenate | solution.py:98
  142.4 1.9 fusion.1
  144.3 3.0 fusion.27
  147.3 4.5 all-reduce.3
  154.5 2.3 convolution_reduce_fusion
  158.0 1.7 copy-done.3
  159.8 1.9 slice_bitcast_fusion
  161.6 3.1 broadcast_in_dim.66
  164.7 18.4 %scatter_fusion = f32[256,8,768]{2,1,0:T(8,128)} fusion(f32[256,8,768]{2,1,0:T(8,128)} %broadcast_in_dim.66, s32[128]{0:T(128)S(1)} %get-tuple-element.37, f32[128,8,768]{2,1,0:T(8,128)} %slice_bitcast_fusion), kind=kCustom, calls=%fused_computation.2 | custom fusion | bytes 9437696 | tf_op jit(solution)/shard_map/scatter | solution.py:127
  183.1 10.3 %all-to-all-start.2 = ((f32[128,2,8,768]{3,2,1,0:T(8,128)}), f32[128,2,8,768]{3,2,1,0:T(8,128)}, u32[]{:S(2)}, u32[]{:S(2)}) async-start(f32[128,2,8,768]{3,2,1,0:T(8,128)} %bitcast.64), calls=%async_computation.3 | async-start | bytes 12582912 | tf_op jit(solution)/shard_map/all_to_all | solution.py:128
  194.0 2.4 all_gather.9
  196.3 4.4 multiply_reduce_fusion
  202.5 1.3 stack.31
  203.9 2.9 fusion.12
  206.8 490.5 %fusion = f32[16,768]{1,0:T(8,128)S(1)} fusion(f32[1536,768]{1,0:T(8,128)} %fusion.12), kind=kCustom, calls=%all-reduce-scatter | all-reduce-scatter fusion | flops 1572865 | bytes 4768768
  697.3 1.3 collective-permute-start.30
  698.6 1.3 collective-permute-start.31
  699.9 1.3 collective-permute-start.29
  701.2 1.3 collective-permute-start.28
  702.5 31.5 %collective-permute-start.27 = (f32[16,768]{1,0:T(8,128)S(1)}, f32[16,768]{1,0:T(8,128)S(1)}, u32[]{:S(2)}, u32[]{:S(2)}) collective-permute-start(f32[16,768]{1,0:T(8,128)S(1)} %fusion), channel_id=1, source_target_pairs={{0,56},{2,58},{4,60},{6,62},{8,64},{10,66},{12,68},{14,70},{16,72}... | collective-permute-start | bytes 147464
  734.0 1.3 collective-permute-start.26
  735.3 1.3 collective-permute-start.25
  736.6 1.3 collective-permute-start.24
  737.9 1.3 collective-permute-start.23
  739.2 1.3 collective-permute-start.22
  740.5 1.3 collective-permute-start.21
  741.9 7.2 collective-permute-start.20
  749.1 5.4 collective-permute-start.19
  754.5 4.2 collective-permute-start.18
  758.7 1.3 collective-permute-start.17
  760.0 4.8 collective-permute-start.16
  764.9 1.3 collective-permute-start.15
  766.2 2.0 collective-permute-start.14
  768.2 3.2 collective-permute-start.13
  771.4 4.6 collective-permute-start.12
  776.0 4.1 collective-permute-start.11
  780.2 2.2 collective-permute-start.10
  782.4 4.4 collective-permute-start.9
  786.8 3.2 collective-permute-start.8
  790.0 1.9 collective-permute-start.7
  792.0 3.7 collective-permute-start.6
  795.7 2.8 collective-permute-start.5
  798.5 4.4 collective-permute-start.4
  803.0 3.9 collective-permute-start.3
  806.9 3.2 collective-permute-start.2
  810.1 4.6 collective-permute-start.1
  814.7 2.1 collective-permute-start
  819.7 3.2 collective-permute-done
  822.9 47.2 %concatenate.4 = f32[524,768]{1,0:T(8,128)} concatenate(f32[12,768]{1,0:T(8,128)S(1)} %collective-permute-done.31, f32[16,768]{1,0:T(8,128)S(1)} %collective-permute-done.30, f32[16,768]{1,0:T(8,128)S(1)} %collective-permute-done.29, f32[16,768]{1,0:T(8,128)S(1)} %collective-permute-done.28, f32[16,768]{1,0:T(8,128)S(1)} %collective-permute-done.27, ...), dimensions={0} | concatenate | bytes 3219456
  870.1 1.5 dynamic-slice_multiply_fusion
  871.6 2.2 reduce_sum.162
  874.4 5.4 copy.27
  879.8 2.2 fusion.16
  882.0 1.8 slice_add_fusion
  (123 shorter events, 15.0 us)
Async XLA Ops:
  7.2 46.8 %copy-start = (bf16[1536,768]{1,0:T(8,128)(2,1)S(1)}, bf16[1536,768]{1,0:T(8,128)(2,1)}, u32[]{:S(2)}) copy-start(bf16[1536,768]{1,0:T(8,128)(2,1)} %param.9) | copy-start | bytes 7077892
  36.9 4.0 copy-start.7
  44.3 8.0 copy-start.6
  44.4 8.1 copy-start.16
  44.4 80.7 %all-to-all-start.1 = ((bf16[128,2,8,768]{3,2,1,0:T(8,128)(2,1)}), bf16[128,2,8,768]{3,2,1,0:T(8,128)(2,1)}, u32[]{:S(2)}, u32[]{:S(2)}) async-start(bf16[128,2,8,768]{3,2,1,0:T(8,128)(2,1)} %select_select_fusion), calls=%async_computation.2 | async-start | bytes 6291456 | tf_op jit(solution)/shard_map/all_to_all | solution.py:88
  52.3 19.7 %reduce-scatter.4.cloned.1.call-start = ((), (), s32[]{:S(2)}) async-start(), calls=%async_computation.4 | async-start | bytes 2359296 | tf_op jit(solution)/shard_map/reduce_scatter | solution.py:65
  52.4 0.9 copy-start.4
  54.0 2.0 copy-start.17
  125.0 6.5 copy-start.1
  125.0 6.5 copy-start.18
  151.7 5.8 copy-start.2
  158.0 1.7 copy-start.3
  183.1 10.3 %copy-start.5 = (f32[256,768]{1,0:T(8,128)S(1)}, f32[256,768]{1,0:T(8,128)}, u32[]{:S(2)}) copy-start(f32[256,768]{1,0:T(8,128)} %reduce-scatter.4.cloned.1.call-done) | copy-start | bytes 2359300
  183.1 691.3 %all-to-all-start.2 = ((f32[128,2,8,768]{3,2,1,0:T(8,128)}), f32[128,2,8,768]{3,2,1,0:T(8,128)}, u32[]{:S(2)}, u32[]{:S(2)}) async-start(f32[128,2,8,768]{3,2,1,0:T(8,128)} %bitcast.64), calls=%async_computation.3 | async-start | bytes 12582912 | tf_op jit(solution)/shard_map/all_to_all | solution.py:128
  193.4 678.2 %all-gather.4.cloned.1.call-start = ((), (), s32[]{:S(2)}) async-start(), calls=%async_computation.5 | async-start | bytes 3170304 | tf_op jit(solution)/shard_map/all_gather | solution.py:16
  206.8 610.1 %copy-start.19 = (u32[256]{0:T(256)S(1)}, u32[256]{0:T(256)}, u32[]{:S(2)}) copy-start(u32[256]{0:T(256)} %constant.94) | copy-start | bytes 3076
  206.8 611.9 %copy-start.8 = (s32[128,1,2]{2,1,0:T(1,128)S(1)}, s32[128,1,2]{2,1,0:T(1,128)}, u32[]{:S(2)}) copy-start(s32[128,1,2]{2,1,0:T(1,128)} %copy-done.7) | copy-start | bytes 3076
  697.3 38.0 %collective-permute-start.30 = (f32[16,768]{1,0:T(8,128)S(1)}, f32[16,768]{1,0:T(8,128)S(1)}, u32[]{:S(2)}, u32[]{:S(2)}) collective-permute-start(f32[16,768]{1,0:T(8,128)S(1)} %fusion), channel_id=1, source_target_pairs={{0,62},{2,64},{4,66},{6,68},{8,70},{10,72},{12,74},{14,76},{16,78}... | collective-permute-start | bytes 147464
  698.6 35.4 %collective-permute-start.31 = (f32[12,768]{1,0:T(8,128)S(1)}, f32[12,768]{1,0:T(8,128)S(1)}, u32[]{:S(2)}, u32[]{:S(2)}) collective-permute-start(f32[12,768]{1,0:T(8,128)S(1)} %slice.74), channel_id=1, source_target_pairs={{0,64},{2,66},{4,68},{6,70},{8,72},{10,74},{12,76},{14,78},{16,80}... | collective-permute-start | bytes 110600
  699.9 36.7 %collective-permute-start.29 = (f32[16,768]{1,0:T(8,128)S(1)}, f32[16,768]{1,0:T(8,128)S(1)}, u32[]{:S(2)}, u32[]{:S(2)}) collective-permute-start(f32[16,768]{1,0:T(8,128)S(1)} %fusion), channel_id=1, source_target_pairs={{0,60},{2,62},{4,64},{6,66},{8,68},{10,70},{12,72},{14,74},{16,76}... | collective-permute-start | bytes 147464
  701.2 36.7 %collective-permute-start.28 = (f32[16,768]{1,0:T(8,128)S(1)}, f32[16,768]{1,0:T(8,128)S(1)}, u32[]{:S(2)}, u32[]{:S(2)}) collective-permute-start(f32[16,768]{1,0:T(8,128)S(1)} %fusion), channel_id=1, source_target_pairs={{0,58},{2,60},{4,62},{6,64},{8,66},{10,68},{12,70},{14,72},{16,74}... | collective-permute-start | bytes 147464
  702.5 36.7 %collective-permute-start.27 = (f32[16,768]{1,0:T(8,128)S(1)}, f32[16,768]{1,0:T(8,128)S(1)}, u32[]{:S(2)}, u32[]{:S(2)}) collective-permute-start(f32[16,768]{1,0:T(8,128)S(1)} %fusion), channel_id=1, source_target_pairs={{0,56},{2,58},{4,60},{6,62},{8,64},{10,66},{12,68},{14,70},{16,72}... | collective-permute-start | bytes 147464
  734.0 6.5 collective-permute-start.26
  735.3 6.5 collective-permute-start.25
  736.6 12.4 %collective-permute-start.24 = (f32[16,768]{1,0:T(8,128)S(1)}, f32[16,768]{1,0:T(8,128)S(1)}, u32[]{:S(2)}, u32[]{:S(2)}) collective-permute-start(f32[16,768]{1,0:T(8,128)S(1)} %fusion), channel_id=1, source_target_pairs={{0,50},{2,52},{4,54},{6,56},{8,58},{10,60},{12,62},{14,64},{16,66}... | collective-permute-start | bytes 147464
  737.9 16.6 %collective-permute-start.23 = (f32[16,768]{1,0:T(8,128)S(1)}, f32[16,768]{1,0:T(8,128)S(1)}, u32[]{:S(2)}, u32[]{:S(2)}) collective-permute-start(f32[16,768]{1,0:T(8,128)S(1)} %fusion), channel_id=1, source_target_pairs={{0,48},{2,50},{4,52},{6,54},{8,56},{10,58},{12,60},{14,62},{16,64}... | collective-permute-start | bytes 147464
  739.2 19.5 %collective-permute-start.22 = (f32[16,768]{1,0:T(8,128)S(1)}, f32[16,768]{1,0:T(8,128)S(1)}, u32[]{:S(2)}, u32[]{:S(2)}) collective-permute-start(f32[16,768]{1,0:T(8,128)S(1)} %fusion), channel_id=1, source_target_pairs={{0,46},{2,48},{4,50},{6,52},{8,54},{10,56},{12,58},{14,60},{16,62}... | collective-permute-start | bytes 147464
  740.5 19.5 %collective-permute-start.21 = (f32[16,768]{1,0:T(8,128)S(1)}, f32[16,768]{1,0:T(8,128)S(1)}, u32[]{:S(2)}, u32[]{:S(2)}) collective-permute-start(f32[16,768]{1,0:T(8,128)S(1)} %fusion), channel_id=1, source_target_pairs={{0,44},{2,46},{4,48},{6,50},{8,52},{10,54},{12,56},{14,58},{16,60}... | collective-permute-start | bytes 147464
  741.9 23.0 %collective-permute-start.20 = (f32[16,768]{1,0:T(8,128)S(1)}, f32[16,768]{1,0:T(8,128)S(1)}, u32[]{:S(2)}, u32[]{:S(2)}) collective-permute-start(f32[16,768]{1,0:T(8,128)S(1)} %fusion), channel_id=1, source_target_pairs={{0,42},{2,44},{4,46},{6,48},{8,50},{10,52},{12,54},{14,56},{16,58}... | collective-permute-start | bytes 147464
  749.1 17.1 %collective-permute-start.19 = (f32[16,768]{1,0:T(8,128)S(1)}, f32[16,768]{1,0:T(8,128)S(1)}, u32[]{:S(2)}, u32[]{:S(2)}) collective-permute-start(f32[16,768]{1,0:T(8,128)S(1)} %fusion), channel_id=1, source_target_pairs={{0,40},{2,42},{4,44},{6,46},{8,48},{10,50},{12,52},{14,54},{16,56}... | collective-permute-start | bytes 147464
  754.5 13.7 %collective-permute-start.18 = (f32[16,768]{1,0:T(8,128)S(1)}, f32[16,768]{1,0:T(8,128)S(1)}, u32[]{:S(2)}, u32[]{:S(2)}) collective-permute-start(f32[16,768]{1,0:T(8,128)S(1)} %fusion), channel_id=1, source_target_pairs={{0,38},{2,40},{4,42},{6,44},{8,46},{10,48},{12,50},{14,52},{16,54}... | collective-permute-start | bytes 147464
  758.7 12.7 %collective-permute-start.17 = (f32[16,768]{1,0:T(8,128)S(1)}, f32[16,768]{1,0:T(8,128)S(1)}, u32[]{:S(2)}, u32[]{:S(2)}) collective-permute-start(f32[16,768]{1,0:T(8,128)S(1)} %fusion), channel_id=1, source_target_pairs={{0,36},{2,38},{4,40},{6,42},{8,44},{10,46},{12,48},{14,50},{16,52}... | collective-permute-start | bytes 147464
  760.0 16.0 %collective-permute-start.16 = (f32[16,768]{1,0:T(8,128)S(1)}, f32[16,768]{1,0:T(8,128)S(1)}, u32[]{:S(2)}, u32[]{:S(2)}) collective-permute-start(f32[16,768]{1,0:T(8,128)S(1)} %fusion), channel_id=1, source_target_pairs={{0,34},{2,36},{4,38},{6,40},{8,42},{10,44},{12,46},{14,48},{16,50}... | collective-permute-start | bytes 147464
  764.9 15.3 %collective-permute-start.15 = (f32[16,768]{1,0:T(8,128)S(1)}, f32[16,768]{1,0:T(8,128)S(1)}, u32[]{:S(2)}, u32[]{:S(2)}) collective-permute-start(f32[16,768]{1,0:T(8,128)S(1)} %fusion), channel_id=1, source_target_pairs={{0,32},{2,34},{4,36},{6,38},{8,40},{10,42},{12,44},{14,46},{16,48}... | collective-permute-start | bytes 147464
  766.2 16.2 %collective-permute-start.14 = (f32[16,768]{1,0:T(8,128)S(1)}, f32[16,768]{1,0:T(8,128)S(1)}, u32[]{:S(2)}, u32[]{:S(2)}) collective-permute-start(f32[16,768]{1,0:T(8,128)S(1)} %fusion), channel_id=1, source_target_pairs={{0,30},{2,32},{4,34},{6,36},{8,38},{10,40},{12,42},{14,44},{16,46}... | collective-permute-start | bytes 147464
  768.2 18.6 %collective-permute-start.13 = (f32[16,768]{1,0:T(8,128)S(1)}, f32[16,768]{1,0:T(8,128)S(1)}, u32[]{:S(2)}, u32[]{:S(2)}) collective-permute-start(f32[16,768]{1,0:T(8,128)S(1)} %fusion), channel_id=1, source_target_pairs={{0,28},{2,30},{4,32},{6,34},{8,36},{10,38},{12,40},{14,42},{16,44}... | collective-permute-start | bytes 147464
  771.4 18.6 %collective-permute-start.12 = (f32[16,768]{1,0:T(8,128)S(1)}, f32[16,768]{1,0:T(8,128)S(1)}, u32[]{:S(2)}, u32[]{:S(2)}) collective-permute-start(f32[16,768]{1,0:T(8,128)S(1)} %fusion), channel_id=1, source_target_pairs={{0,26},{2,28},{4,30},{6,32},{8,34},{10,36},{12,38},{14,40},{16,42}... | collective-permute-start | bytes 147464
  776.0 15.9 %collective-permute-start.11 = (f32[16,768]{1,0:T(8,128)S(1)}, f32[16,768]{1,0:T(8,128)S(1)}, u32[]{:S(2)}, u32[]{:S(2)}) collective-permute-start(f32[16,768]{1,0:T(8,128)S(1)} %fusion), channel_id=1, source_target_pairs={{0,24},{2,26},{4,28},{6,30},{8,32},{10,34},{12,36},{14,38},{16,40}... | collective-permute-start | bytes 147464
  780.2 15.5 %collective-permute-start.10 = (f32[16,768]{1,0:T(8,128)S(1)}, f32[16,768]{1,0:T(8,128)S(1)}, u32[]{:S(2)}, u32[]{:S(2)}) collective-permute-start(f32[16,768]{1,0:T(8,128)S(1)} %fusion), channel_id=1, source_target_pairs={{0,22},{2,24},{4,26},{6,28},{8,30},{10,32},{12,34},{14,36},{16,38}... | collective-permute-start | bytes 147464
  782.4 16.1 %collective-permute-start.9 = (f32[16,768]{1,0:T(8,128)S(1)}, f32[16,768]{1,0:T(8,128)S(1)}, u32[]{:S(2)}, u32[]{:S(2)}) collective-permute-start(f32[16,768]{1,0:T(8,128)S(1)} %fusion), channel_id=1, source_target_pairs={{0,20},{2,22},{4,24},{6,26},{8,28},{10,30},{12,32},{14,34},{16,36}... | collective-permute-start | bytes 147464
  786.8 16.1 %collective-permute-start.8 = (f32[16,768]{1,0:T(8,128)S(1)}, f32[16,768]{1,0:T(8,128)S(1)}, u32[]{:S(2)}, u32[]{:S(2)}) collective-permute-start(f32[16,768]{1,0:T(8,128)S(1)} %fusion), channel_id=1, source_target_pairs={{0,18},{2,20},{4,22},{6,24},{8,26},{10,28},{12,30},{14,32},{16,34}... | collective-permute-start | bytes 147464
  790.0 16.8 %collective-permute-start.7 = (f32[16,768]{1,0:T(8,128)S(1)}, f32[16,768]{1,0:T(8,128)S(1)}, u32[]{:S(2)}, u32[]{:S(2)}) collective-permute-start(f32[16,768]{1,0:T(8,128)S(1)} %fusion), channel_id=1, source_target_pairs={{0,16},{2,18},{4,20},{6,22},{8,24},{10,26},{12,28},{14,30},{16,32}... | collective-permute-start | bytes 147464
  791.9 26.2 %copy-start.9 = (f32[16,768]{1,0:T(8,128)}, f32[16,768]{1,0:T(8,128)S(1)}, u32[]{:S(2)}) copy-start(f32[16,768]{1,0:T(8,128)S(1)} %collective-permute-done.11) | copy-start | bytes 147460
  792.0 18.1 %collective-permute-start.6 = (f32[16,768]{1,0:T(8,128)S(1)}, f32[16,768]{1,0:T(8,128)S(1)}, u32[]{:S(2)}, u32[]{:S(2)}) collective-permute-start(f32[16,768]{1,0:T(8,128)S(1)} %fusion), channel_id=1, source_target_pairs={{0,14},{2,16},{4,18},{6,20},{8,22},{10,24},{12,26},{14,28},{16,30}... | collective-permute-start | bytes 147464
  795.7 19.0 %copy-start.10 = (f32[16,768]{1,0:T(8,128)}, f32[16,768]{1,0:T(8,128)S(1)}, u32[]{:S(2)}) copy-start(f32[16,768]{1,0:T(8,128)S(1)} %collective-permute-done.10) | copy-start | bytes 147460
  795.7 19.0 %collective-permute-start.5 = (f32[16,768]{1,0:T(8,128)S(1)}, f32[16,768]{1,0:T(8,128)S(1)}, u32[]{:S(2)}, u32[]{:S(2)}) collective-permute-start(f32[16,768]{1,0:T(8,128)S(1)} %fusion), channel_id=1, source_target_pairs={{0,12},{2,14},{4,16},{6,18},{8,20},{10,22},{12,24},{14,26},{16,28}... | collective-permute-start | bytes 147464
  798.5 18.4 %copy-start.11 = (f32[16,768]{1,0:T(8,128)}, f32[16,768]{1,0:T(8,128)S(1)}, u32[]{:S(2)}) copy-start(f32[16,768]{1,0:T(8,128)S(1)} %collective-permute-done.9) | copy-start | bytes 147460
  798.5 21.1 %collective-permute-start.4 = (f32[16,768]{1,0:T(8,128)S(1)}, f32[16,768]{1,0:T(8,128)}, u32[]{:S(2)}, u32[]{:S(2)}) collective-permute-start(f32[16,768]{1,0:T(8,128)S(1)} %fusion), channel_id=1, source_target_pairs={{0,10},{2,12},{4,14},{6,16},{8,18},{10,20},{12,22},{14,24},{16,26}... | collective-permute-start | bytes 147464
  802.9 13.9 %copy-start.12 = (f32[16,768]{1,0:T(8,128)}, f32[16,768]{1,0:T(8,128)S(1)}, u32[]{:S(2)}) copy-start(f32[16,768]{1,0:T(8,128)S(1)} %collective-permute-done.8) | copy-start | bytes 147460
  803.0 16.7 %collective-permute-start.3 = (f32[16,768]{1,0:T(8,128)S(1)}, f32[16,768]{1,0:T(8,128)}, u32[]{:S(2)}, u32[]{:S(2)}) collective-permute-start(f32[16,768]{1,0:T(8,128)S(1)} %fusion), channel_id=1, source_target_pairs={{0,8},{2,10},{4,12},{6,14},{8,16},{10,18},{12,20},{14,22},{16,24},... | collective-permute-start | bytes 147464
  806.8 10.1 %copy-start.13 = (f32[16,768]{1,0:T(8,128)}, f32[16,768]{1,0:T(8,128)S(1)}, u32[]{:S(2)}) copy-start(f32[16,768]{1,0:T(8,128)S(1)} %collective-permute-done.7) | copy-start | bytes 147460
  806.9 12.8 %collective-permute-start.2 = (f32[16,768]{1,0:T(8,128)S(1)}, f32[16,768]{1,0:T(8,128)}, u32[]{:S(2)}, u32[]{:S(2)}) collective-permute-start(f32[16,768]{1,0:T(8,128)S(1)} %fusion), channel_id=1, source_target_pairs={{0,6},{2,8},{4,10},{6,12},{8,14},{10,16},{12,18},{14,20},{16,22},{... | collective-permute-start | bytes 147464
  810.1 6.8 copy-start.14
  810.1 9.6 %collective-permute-start.1 = (f32[16,768]{1,0:T(8,128)S(1)}, f32[16,768]{1,0:T(8,128)}, u32[]{:S(2)}, u32[]{:S(2)}) collective-permute-start(f32[16,768]{1,0:T(8,128)S(1)} %fusion), channel_id=1, source_target_pairs={{0,4},{2,6},{4,8},{6,10},{8,12},{10,14},{12,16},{14,18},{16,20},{1... | collective-permute-start | bytes 147464
  814.7 2.2 copy-start.15
  814.7 8.2 collective-permute-start
Sparse Core Ops, SparseCore 0:
  56.1 15.8 reduce-scatter.3
  204.0 139.2 all-gather.3
